TPU v7x, 32 devices: a whole 2x2x4 slice. The times are simulated.
32 devices in a mesh: vol: 4 (over y, core), sec: 8 (over z, x).
Axes of the slice: x: 2, y: 2, z: 4, core: 2. Of those that a mesh axis runs over, the one named last changes fastest.
Arguments:
- rhs: float32 [64, 8, 64, 1024], P(None, None, 'vol', 'sec'), may hold values from -6 to 6
- flux_in: float32 [64, 64, 1024], P(None, 'vol', 'sec'), may hold values from -12 to 12
- materials: int32 [8, 64, 1024], P(None, 'vol', 'sec'), may hold values from 0 to 7
- mat_coef: float32 [8], replicated, may hold values from 0.5 to 4
- owner_perm: int32 [8], replicated, may hold values from 0 to 7, each once
- blocks: bfloat16 [8, 8192, 8192], P('sec', None, 'vol'), may hold values from -0.0625 to 0.0625
Outputs:
- solution: float32 [64, 8, 64, 1024], P(None, None, 'vol', 'sec')
- flux_out: float32 [64, 64, 1024], P(None, 'vol', 'sec')
Inputs may be any that keep to these rules, and one draw needn't show every extreme that they name: `owner_perm`: every harmonic index appears once.
All inputs are finite; a program needn't handle non-finite values.
Results may differ from a plain program's by a relative error of at most 0.008.
Values may be sent and summed in bfloat16 or wider, within the bound.
A program may use at most 128 MiB of HBM per device.

v0:
```python
import functools
import math

import jax
import jax.numpy as jnp
import numpy as np
from jax import lax
from jax.experimental import pallas as pl
from jax.experimental.pallas import tpu as pltpu
from jax.sharding import PartitionSpec as P

SWEEPS = 4
HALVES = 2
CHUNK = 16
GROUP = 4
MESH = pl.DeviceIdType.MESH
F32, BF16 = jnp.float32, jnp.bfloat16

center = 1.0
radius = 0.93


def basis_table(count):
    harm = np.arange(count)[:, None]
    sect = np.arange(count)[None, :]
    mid = count // 2
    wave = np.where(harm <= mid, harm, harm - mid)
    phase = 2.0 * np.pi * (wave * sect % count) / count
    value = np.where(harm <= mid, np.cos(phase), np.sin(phase))
    ends = (harm == 0) | (harm == mid)
    return (value * np.where(ends, math.sqrt(1.0 / count), math.sqrt(2.0 / count))).astype(np.float32)


def neighbour_matrices(depth, axial, pts):
    rows = depth * axial
    d, z = np.divmod(np.arange(rows), axial)
    same_d = d[:, None] == d[None, :]
    same_z = z[:, None] == z[None, :]
    near = (same_d & (abs(z[:, None] - z[None, :]) == 1)) | (
        same_z & (abs(d[:, None] - d[None, :]) == 1)
    )
    out = np.zeros((2, rows, rows + 4 * depth), np.float32)
    out[:, :, :rows] = near
    for j in range(2):
        for layer in range(depth):
            out[j, layer * axial, rows + j * depth + layer] = 1.0
            out[j, layer * axial + axial - 1, rows + 2 * depth + j * depth + layer] = 1.0
    p = np.arange(pts)
    shift = (abs(p[:, None] - p[None, :]) == 1).astype(np.float32)
    return jnp.asarray(out, BF16), jnp.asarray(shift, BF16)


def kernel(
    sizes,
    rhs, flux_in, mats, coef, perm, table, near, shift, blocks,
    sol_out, flux_out,
    bl, res, dirn, sol, fin, inv, fout,
    ax_send, ax_recv, co_send, co_recv,
    traces, resp, part_send, part_recv, harm, acc,
    in_sem, bl_sem, out_sem, fo_sem,
    axs_sem, axr_sem, cos_sem, cor_sem,
    raws_sem, rawr_sem, ps_sem, pr_sem, hs_sem, hr_sem,
):
    exc, depth, axial, pts, nv, ns, nmat = sizes
    rows = depth * axial
    chunks = exc // CHUNK
    per_half = chunks // HALVES
    eh = exc // HALVES
    crow = CHUNK * rows
    groups = ns // GROUP
    steps = SWEEPS - 1
    v = lax.axis_index("vol")
    s = lax.axis_index("sec")
    up, down = lax.rem(v + 1, nv), lax.rem(v + nv - 1, nv)
    right, left = lax.rem(s + 1, ns), lax.rem(s + ns - 1, ns)
    low = lax.rem(s, GROUP)
    grp = s // GROUP
    mate2 = s + 2 - 4 * lax.rem(s // 2, 2)
    mate1 = s + 1 - 2 * lax.rem(s, 2)
    low2 = lax.rem(mate2, GROUP)

    load = []
    flux_load = pltpu.make_async_copy(flux_in, fin, in_sem.at[chunks])
    flux_load.start()
    for c in range(chunks):
        cp = pltpu.make_async_copy(
            rhs.at[pl.ds(c * crow, crow)], res.at[pl.ds(c * crow, crow)], in_sem.at[c]
        )
        cp.start()
        load.append(cp)
    kv = axial * pts
    bl_load = pltpu.make_async_copy(blocks, bl, bl_sem)
    bl_load.start()

    barrier = pltpu.get_barrier_semaphore()
    greet = [(lax.rem(v + k, nv), s) for k in range(1, nv)]
    greet += [(v, right), (v, left), (v, mate1), (v, mate2)]
    greet += [(v, lax.rem(grp + k, groups) * GROUP + low) for k in range(1, groups)]
    for dev in greet:
        pl.semaphore_signal(barrier, inc=1, device_id=dev, device_id_type=MESH)

    sigma = jnp.zeros((rows, pts), F32)
    ids = mats[...]
    for m in range(nmat):
        sigma = jnp.where(ids == m, coef[m], sigma)
    inv[...] = 1.0 / (6.0 + sigma)

    def remote(src, dst, ssem, rsem, dev):
        return pltpu.make_async_remote_copy(
            src_ref=src, dst_ref=dst, send_sem=ssem, recv_sem=rsem,
            device_id=dev, device_id_type=MESH,
        )

    pending = []
    row2 = lax.broadcasted_iota(jnp.int32, (2 * CHUNK, pts), 0)
    lane2 = lax.broadcasted_iota(jnp.int32, (2 * CHUNK, pts), 1)

    def picker(e, first, second):
        hit = ((row2 == e) & (lane2 == first)) | ((row2 == e + CHUNK) & (lane2 == second))
        return jnp.where(hit, 1.0, 0.0).astype(BF16)

    def pack(e, xb):
        return lax.dot_general(
            picker(e, pts - 1, 0), xb, (((1,), (1,)), ((), ())), preferred_element_type=F32
        )

    halo = {}

    def send_halo(k, c, packed):
        base = c * crow
        n = CHUNK * depth
        ax_send[k, c, 0] = dirn[pl.ds(base + axial - 1, n, stride=axial), :].astype(BF16)
        ax_send[k, c, 1] = dirn[pl.ds(base, n, stride=axial), :].astype(BF16)
        co_send[k, c, 0] = packed[:CHUNK].astype(BF16)
        co_send[k, c, 1] = packed[CHUNK:].astype(BF16)
        cps = []
        for i, (vd, sd) in enumerate(((up, right), (down, left))):
            cps.append(remote(ax_send.at[k, c, i], ax_recv.at[k, c, i],
                              axs_sem.at[k, c, i], axr_sem.at[k, c, i], (vd, s)))
            cps.append(remote(co_send.at[k, c, i], co_recv.at[k, c, i],
                              cos_sem.at[k, c, i], cor_sem.at[k, c, i], (v, sd)))
        for cp in cps:
            cp.start()
        halo[k, c] = cps

    flux_load.wait()
    waited = False
    for c in range(chunks):
        load[c].wait()

        def first(e, packed, c=c):
            at = pl.multiple_of(c * crow + e * rows, rows)
            top = pl.ds(at + (depth - 1) * axial, axial)
            fat = pl.multiple_of((c * CHUNK + e) * axial, axial)
            res[top, :] = res[top, :] + fin[pl.ds(fat, axial), :]
            here = pl.ds(at, rows)
            x = res[here, :] * inv[...]
            res[here, :] = x
            x = x / center
            dirn[here, :] = x
            sol[here, :] = x
            return packed + pack(e, x.astype(BF16))

        packed = lax.fori_loop(0, CHUNK, first, jnp.zeros((2 * CHUNK, rows), F32))
        if not waited:
            pl.semaphore_wait(barrier, len(greet))
            waited = True
        send_halo(0, c, packed)

    sigma_one = center / radius
    ratios = [1.0 / sigma_one]
    for _ in range(steps):
        ratios.append(1.0 / (2.0 * sigma_one - ratios[-1]))

    outs = []

    def sweep(k, c):
        for cp in halo[k, c]:
            cp.wait_recv()
        pending.extend(halo[k, c])
        a = ratios[k + 1] * ratios[k]
        b = 2.0 * ratios[k + 1] / radius
        cols = jnp.concatenate(
            [co_recv[k, c, 0].astype(F32), co_recv[k, c, 1].astype(F32)], axis=0
        ).T.astype(BF16)
        last = k + 1 == steps

        def pair(q, packed):
            hrow = pl.ds(pl.multiple_of(q * 2 * depth, 2 * depth), 2 * depth)
            lo = ax_recv[k, c, 0, hrow, :]
            hi = ax_recv[k, c, 1, hrow, :]
            for j in range(2):
                e = q * 2 + j
                here = pl.ds(pl.multiple_of(c * crow + e * rows, rows), rows)
                x = dirn[here, :]
                xb = x.astype(BF16)
                tot = jnp.dot(near[j], jnp.concatenate([xb, lo, hi], axis=0),
                              preferred_element_type=F32)
                tot = tot + jnp.dot(
                    jnp.concatenate([xb, cols], axis=1),
                    jnp.concatenate([shift[...], picker(e, 0, pts - 1)], axis=0),
                    preferred_element_type=F32)
                r = res[here, :] - x + inv[...] * tot
                y = a * x + b * r
                sol[here, :] = sol[here, :] + y
                if not last:
                    res[here, :] = r
                    dirn[here, :] = y
                    packed = packed + pack(e, y.astype(BF16))
            return packed

        packed = lax.fori_loop(0, CHUNK // 2, pair, jnp.zeros((2 * CHUNK, rows), F32))
        if not last:
            send_halo(k + 1, c, packed)
        else:
            cp = pltpu.make_async_copy(
                sol.at[pl.ds(c * crow, crow)], sol_out.at[pl.ds(c * crow, crow)], out_sem.at[c]
            )
            cp.start()
            outs.append(cp)
            h, off = c // per_half, (c % per_half) * CHUNK
            for z in range(axial):
                got = sol[pl.ds(c * crow + (depth - 1) * axial + z, CHUNK, stride=rows), :]
                traces[h, low, z, off:off + CHUNK, :] = got.astype(BF16)

    def weight(way, target, member):
        if way == 0:
            return table[perm[target], member]
        return table[perm[member], target]

    raw = (traces, resp)
    state = {}

    def mix(way, h, target, finish):
        ws = [weight(way, target, grp * GROUP + m) for m in range(GROUP)]

        def one(z, carry):
            total = ws[0] * raw[way][h, 0, z].astype(F32)
            for m in range(1, GROUP):
                total = total + ws[m] * raw[way][h, m, z].astype(F32)
            finish(z, total)
            return carry

        lax.fori_loop(0, axial, one, 0)

    def raw_copy(way, h, slot, i, dev):
        ref = raw[way].at[h, slot]
        return remote(ref, ref, raws_sem.at[way, h, i], rawr_sem.at[way, h, i], dev)

    def fold1(way, h):
        cp = raw_copy(way, h, low, 0, (v, mate2))
        cq = raw_copy(way, h, low, 1, (v, mate1))
        cp.start()
        cq.start()
        state[way, h] = [cp, cq]

    def fold2(way, h):
        state[way, h][0].wait_recv()
        cr = raw_copy(way, h, low2, 2, (v, mate1))
        cr.start()
        state[way, h].append(cr)

    def fold3(way, h):
        state[way, h][1].wait_recv()
        state[way, h][2].wait_recv()
        pending.extend(state[way, h])
        state[way, h] = []
        for k in range(1, groups):
            target = lax.rem(grp + k, groups) * GROUP + low

            def put(z, total, k=k):
                part_send[way, h, k - 1, z] = total.astype(BF16)

            mix(way, h, target, put)
            cp = remote(part_send.at[way, h, k - 1], part_recv.at[way, h, k - 1],
                        ps_sem.at[way, h, k - 1], pr_sem.at[way, h, k - 1], (v, target))
            cp.start()
            state[way, h].append(cp)

    def fold_end(way, h, put):
        for cp in state[way, h]:
            cp.wait_recv()
        pending.extend(state[way, h])

        def finish(z, total):
            for k in range(1, groups):
                total = total + part_recv[way, h, k - 1, z].astype(F32)
            put(z, total)

        mix(way, h, s, finish)

    gathers = {}

    def gather(h):
        def put(z, total):
            harm[h, v, z] = total.astype(BF16)

        fold_end(0, h, put)
        cps = []
        for k in range(1, nv):
            cp = remote(harm.at[h, v], harm.at[h, v], hs_sem.at[h, k - 1], hr_sem.at[h, k - 1],
                        (lax.rem(v + k, nv), s))
            cp.start()
            cps.append(cp)
        gathers[h] = cps

    state["bl"] = False

    def apply(h, k):
        if not state["bl"]:
            bl_load.wait()
            state["bl"] = True
        if k > 0:
            gathers[h][k - 1].wait_recv()
            pending.append(gathers[h][k - 1])
        src = lax.rem(v + nv - k, nv)
        lhs = jnp.concatenate([harm[h, src, z] for z in range(axial)], axis=1)
        zt = min(4, axial)
        krow = pl.ds(pl.multiple_of(src * kv, kv), kv)

        def tile(t, carry):
            col = pl.ds(pl.multiple_of(t * zt * pts, zt * pts), zt * pts)
            got = jnp.dot(lhs, bl[krow, col], preferred_element_type=F32)
            for i in range(zt):
                z = t * zt + i
                piece = got[:, i * pts:(i + 1) * pts]
                if k > 0:
                    piece = piece + acc[z]
                if k + 1 < nv:
                    acc[z] = piece
                else:
                    resp[h, low, z] = piece.astype(BF16)
            return carry

        lax.fori_loop(0, axial // zt, tile, 0)

    def finish_flux(h):
        def put(z, total):
            fout[pl.ds(h * eh * axial + z, eh, stride=axial), :] = total

        fold_end(1, h, put)
        n = eh * axial
        cp = pltpu.make_async_copy(
            fout.at[pl.ds(h * n, n)], flux_out.at[pl.ds(h * n, n)], fo_sem.at[h]
        )
        cp.start()
        outs.append(cp)

    def sweeps(h, k):
        for c in range(h * per_half, (h + 1) * per_half):
            sweep(k, c)

    def run_apply(h, lo, hi):
        for k in range(lo, hi):
            apply(h, k)

    cut = [nv * i // 4 for i in range(5)]
    for k in range(steps):
        sweeps(0, k)
    fold1(0, 0)
    sweeps(1, 0)
    fold2(0, 0)
    sweeps(1, 1)
    fold3(0, 0)
    sweeps(1, 2)
    fold1(0, 1)
    gather(0)
    run_apply(0, cut[0], cut[1])
    fold2(0, 1)
    run_apply(0, cut[1], cut[2])
    fold3(0, 1)
    run_apply(0, cut[2], cut[3])
    gather(1)
    run_apply(0, cut[3], cut[4])
    fold1(1, 0)
    run_apply(1, cut[0], cut[1])
    fold2(1, 0)
    run_apply(1, cut[1], cut[2])
    fold3(1, 0)
    run_apply(1, cut[2], cut[4])
    fold1(1, 1)
    finish_flux(0)
    fold2(1, 1)
    fold3(1, 1)
    finish_flux(1)

    for cp in pending:
        cp.wait_send()
    for cp in outs:
        cp.wait()


def per_device(ns, nv, rhs, flux_in, materials, mat_coef, owner_perm, blocks):
    exc, depth, axial, pts = rhs.shape
    rows = depth * axial
    order, width = blocks.shape[1:]
    chunks = exc // CHUNK
    eh = exc // HALVES
    groups = ns // GROUP
    steps = SWEEPS - 1
    near, shift = neighbour_matrices(depth, axial, pts)
    sizes = (exc, depth, axial, pts, nv, ns, mat_coef.shape[0])
    vm = pl.BlockSpec(memory_space=pltpu.VMEM)
    sm = pl.BlockSpec(memory_space=pltpu.SMEM)
    hb = pl.BlockSpec(memory_space=pl.ANY)
    dma = pltpu.SemaphoreType.DMA
    item = (axial, eh, pts)
    sol, flux = pl.pallas_call(
        functools.partial(kernel, sizes),
        out_shape=(
            jax.ShapeDtypeStruct((exc * rows, pts), F32),
            jax.ShapeDtypeStruct((exc * axial, pts), F32),
        ),
        in_specs=[hb, hb, vm, sm, sm, sm, vm, vm, hb],
        out_specs=(hb, hb),
        scratch_shapes=[
            pltpu.VMEM((order, width), BF16),
            pltpu.VMEM((exc * rows, pts), F32),
            pltpu.VMEM((exc * rows, pts), F32),
            pltpu.VMEM((exc * rows, pts), F32),
            pltpu.VMEM((exc * axial, pts), F32),
            pltpu.VMEM((rows, pts), F32),
            pltpu.VMEM((exc * axial, pts), F32),
            pltpu.VMEM((steps, chunks, 2, CHUNK * depth, pts), BF16),
            pltpu.VMEM((steps, chunks, 2, CHUNK * depth, pts), BF16),
            pltpu.VMEM((steps, chunks, 2, CHUNK, rows), BF16),
            pltpu.VMEM((steps, chunks, 2, CHUNK, rows), BF16),
            pltpu.VMEM((HALVES, GROUP) + item, BF16),
            pltpu.VMEM((HALVES, GROUP) + item, BF16),
            pltpu.VMEM((2, HALVES, groups - 1) + item, BF16),
            pltpu.VMEM((2, HALVES, groups - 1) + item, BF16),
            pltpu.VMEM((HALVES, nv) + item, BF16),
            pltpu.VMEM(item, F32),
            dma((chunks + 1,)), dma, dma((chunks,)), dma((HALVES,)),
            dma((steps, chunks, 2)), dma((steps, chunks, 2)),
            dma((steps, chunks, 2)), dma((steps, chunks, 2)),
            dma((2, HALVES, 3)), dma((2, HALVES, 3)),
            dma((2, HALVES, groups - 1)), dma((2, HALVES, groups - 1)),
            dma((HALVES, nv - 1)), dma((HALVES, nv - 1)),
        ],
        compiler_params=pltpu.CompilerParams(
            collective_id=0, has_side_effects=True, vmem_limit_bytes=60 * 2**20
        ),
        cost_estimate=pl.CostEstimate(
            flops=2 * exc * order * width, bytes_accessed=2 * order * width, transcendentals=0
        ),
    )(
        rhs.reshape(exc * rows, pts),
        flux_in.reshape(exc * axial, pts),
        materials.reshape(rows, pts),
        mat_coef,
        owner_perm,
        jnp.asarray(basis_table(ns)),
        near,
        shift,
        blocks[0],
    )
    return sol.reshape(rhs.shape), flux.reshape(flux_in.shape)


def solution(mesh):
    return jax.shard_map(
        functools.partial(per_device, mesh.shape["sec"], mesh.shape["vol"]),
        mesh=mesh,
        in_specs=(
            P(None, None, "vol", "sec"),
            P(None, "vol", "sec"),
            P(None, "vol", "sec"),
            P(),
            P(),
            P("sec", None, "vol"),
        ),
        out_specs=(P(None, None, "vol", "sec"), P(None, "vol", "sec")),
        check_vma=False,
    )
```

profile of v0, /device:TPU:0, one launch (start us, length us, event | category | flops | bytes accessed | tf_op | source)
XLA Modules:
  0.0 104.1 jit_solution(122165885311833118)
XLA Ops:
  0.6 97.9 %shard_map.104 = (f32[8192,128]{1,0:T(8,128)}, f32[1024,128]{1,0:T(8,128)}) custom-call(f32[8192,128]{1,0:T(8,128)} %bitcast.7, f32[1024,128]{1,0:T(8,128)} %bitcast.9, s32[128,128]{1,0:T(8,128)} %bitcast.11, f32[8]{0:T(128)} %coef.1, s32[8]{0:T(128)} %perm.1, f32[8,8]{1,0:T(8,128)} %constant.8.clone.table, bf16[2,128,160]{2,1,0:T(8,128)(2,1)} %constant.6.clone.near, ...), custom_call_target="tpu_custom_call" | custom-call | flops 2147483648 | bytes 33554432 | tf_op jit(solution)/shard_map/pallas_call | solution.py:408
  98.6 0.0 copy-start
  98.6 4.8 %copy.13 = f32[64,8,16,128]{3,2,1,0:T(8,128)} copy(f32[64,8,16,128]{3,2,1,0:T(8,128)} %bitcast.8) | data formatting | bytes 8388608
  103.3 0.0 copy-done
  103.3 0.8 copy.14
Async XLA Ops:
  98.6 4.8 %copy-start = (f32[1024,128]{1,0:T(8,128)S(1)}, f32[1024,128]{1,0:T(8,128)}, u32[]{:S(2)}) copy-start(f32[1024,128]{1,0:T(8,128)} %get-tuple-element.5) | copy-start | bytes 1572868
where the time goes:
time: 104 us
  Pallas kernels  97.9 us (94%)
  local copies, waits for them, and re-layouts  5.55 us (5%)
    pallas_call x1, Pallas kernels, per_device(): pl.pallas_call(functools.partial(kernel, sizes), out_shape=(jax.ShapeDtyp...  97.9 us
    unnamed x4, local copies, waits for them, and re-layouts  5.55 us

commit v1 on v0

--- a/solution.py
+++ b/solution.py
@@ -47,12 +47,19 @@
             out[j, layer * axial + axial - 1, rows + 2 * depth + j * depth + layer] = 1.0
     p = np.arange(pts)
     shift = (abs(p[:, None] - p[None, :]) == 1).astype(np.float32)
-    return jnp.asarray(out, BF16), jnp.asarray(shift, BF16)
+    sides = np.zeros((2 * CHUNK, pts), np.float32)
+    sides[:CHUNK, 0] = 1.0
+    sides[CHUNK:, pts - 1] = 1.0
+    edges = np.zeros((pts, pts), np.float32)
+    edges[pts - 1, :CHUNK] = 1.0
+    edges[0, CHUNK:2 * CHUNK] = 1.0
+    shift = np.concatenate([shift, sides], axis=0)
+    return jnp.asarray(out, BF16), jnp.asarray(shift, BF16), jnp.asarray(edges, BF16)
 
 
 def kernel(
     sizes,
-    rhs, flux_in, mats, coef, perm, table, near, shift, blocks,
+    rhs, flux_in, mats, coef, perm, table, near, shift, edges, blocks,
     sol_out, flux_out,
     bl, res, dirn, sol, fin, inv, fout,
     ax_send, ax_recv, co_send, co_recv,
@@ -112,17 +119,12 @@
         )
 
     pending = []
-    row2 = lax.broadcasted_iota(jnp.int32, (2 * CHUNK, pts), 0)
-    lane2 = lax.broadcasted_iota(jnp.int32, (2 * CHUNK, pts), 1)
-
-    def picker(e, first, second):
-        hit = ((row2 == e) & (lane2 == first)) | ((row2 == e + CHUNK) & (lane2 == second))
-        return jnp.where(hit, 1.0, 0.0).astype(BF16)
-
-    def pack(e, xb):
-        return lax.dot_general(
-            picker(e, pts - 1, 0), xb, (((1,), (1,)), ((), ())), preferred_element_type=F32
-        )
+    lane = lax.broadcasted_iota(jnp.int32, (rows, pts), 1)
+    side = lax.broadcasted_iota(jnp.int32, (rows, 2 * CHUNK), 1)
+
+    def pack(e, xb, packed):
+        both = jnp.dot(xb, edges[...], preferred_element_type=F32)
+        return jnp.where((lane == e) | (lane == e + CHUNK), both, packed)
 
     halo = {}
 
@@ -131,8 +133,9 @@
         n = CHUNK * depth
         ax_send[k, c, 0] = dirn[pl.ds(base + axial - 1, n, stride=axial), :].astype(BF16)
         ax_send[k, c, 1] = dirn[pl.ds(base, n, stride=axial), :].astype(BF16)
-        co_send[k, c, 0] = packed[:CHUNK].astype(BF16)
-        co_send[k, c, 1] = packed[CHUNK:].astype(BF16)
+        turned = packed.T
+        co_send[k, c, 0] = turned[:CHUNK].astype(BF16)
+        co_send[k, c, 1] = turned[CHUNK:2 * CHUNK].astype(BF16)
         cps = []
         for i, (vd, sd) in enumerate(((up, right), (down, left))):
             cps.append(remote(ax_send.at[k, c, i], ax_recv.at[k, c, i],
@@ -159,9 +162,9 @@
             x = x / center
             dirn[here, :] = x
             sol[here, :] = x
-            return packed + pack(e, x.astype(BF16))
-
-        packed = lax.fori_loop(0, CHUNK, first, jnp.zeros((2 * CHUNK, rows), F32))
+            return pack(e, x.astype(BF16), packed)
+
+        packed = lax.fori_loop(0, CHUNK, first, jnp.zeros((rows, pts), F32))
         if not waited:
             pl.semaphore_wait(barrier, len(greet))
             waited = True
@@ -182,7 +185,7 @@
         b = 2.0 * ratios[k + 1] / radius
         cols = jnp.concatenate(
             [co_recv[k, c, 0].astype(F32), co_recv[k, c, 1].astype(F32)], axis=0
-        ).T.astype(BF16)
+        ).T
         last = k + 1 == steps
 
         def pair(q, packed):
@@ -196,20 +199,19 @@
                 xb = x.astype(BF16)
                 tot = jnp.dot(near[j], jnp.concatenate([xb, lo, hi], axis=0),
                               preferred_element_type=F32)
-                tot = tot + jnp.dot(
-                    jnp.concatenate([xb, cols], axis=1),
-                    jnp.concatenate([shift[...], picker(e, 0, pts - 1)], axis=0),
-                    preferred_element_type=F32)
+                own = jnp.where((side == e) | (side == e + CHUNK), cols, 0.0).astype(BF16)
+                tot = tot + jnp.dot(jnp.concatenate([xb, own], axis=1), shift[...],
+                                    preferred_element_type=F32)
                 r = res[here, :] - x + inv[...] * tot
                 y = a * x + b * r
                 sol[here, :] = sol[here, :] + y
                 if not last:
                     res[here, :] = r
                     dirn[here, :] = y
-                    packed = packed + pack(e, y.astype(BF16))
+                    packed = pack(e, y.astype(BF16), packed)
             return packed
 
-        packed = lax.fori_loop(0, CHUNK // 2, pair, jnp.zeros((2 * CHUNK, rows), F32))
+        packed = lax.fori_loop(0, CHUNK // 2, pair, jnp.zeros((rows, pts), F32))
         if not last:
             send_halo(k + 1, c, packed)
         else:
@@ -398,7 +400,7 @@
     eh = exc // HALVES
     groups = ns // GROUP
     steps = SWEEPS - 1
-    near, shift = neighbour_matrices(depth, axial, pts)
+    near, shift, edges = neighbour_matrices(depth, axial, pts)
     sizes = (exc, depth, axial, pts, nv, ns, mat_coef.shape[0])
     vm = pl.BlockSpec(memory_space=pltpu.VMEM)
     sm = pl.BlockSpec(memory_space=pltpu.SMEM)
@@ -411,7 +413,7 @@
             jax.ShapeDtypeStruct((exc * rows, pts), F32),
             jax.ShapeDtypeStruct((exc * axial, pts), F32),
         ),
-        in_specs=[hb, hb, vm, sm, sm, sm, vm, vm, hb],
+        in_specs=[hb, hb, vm, sm, sm, sm, vm, vm, vm, hb],
         out_specs=(hb, hb),
         scratch_shapes=[
             pltpu.VMEM((order, width), BF16),
@@ -453,6 +455,7 @@
         jnp.asarray(basis_table(ns)),
         near,
         shift,
+        edges,
         blocks[0],
     )
     return sol.reshape(rhs.shape), flux.reshape(flux_in.shape)

time: 104 us -> 110 us (1.058); the launches traced: 104 us -> 109 us
  Pallas kernels: 97.9 us -> 103 us
    pallas_call x1, Pallas kernels: 97.9 us -> 103 us  [per_device(): pl.pallas_call(functools.partial(kernel, sizes), out_shape=(jax.ShapeDtyp...]
where the time goes in v1:
time: 110 us; the launch traced here: 109 us
  Pallas kernels  103 us (94%)
  local copies, waits for them, and re-layouts  5.55 us (5%)
    pallas_call x1, Pallas kernels, per_device(): pl.pallas_call(functools.partial(kernel, sizes), out_shape=(jax.ShapeDtyp...  103 us
    unnamed x4, local copies, waits for them, and re-layouts  5.55 us

profile of v1, /device:TPU:0, one launch (start us, length us, event | category | flops | bytes accessed | tf_op | source)
XLA Modules:
  0.0 108.9 jit_solution(10476595254149597346)
XLA Ops:
  0.6 102.7 %shard_map.113 = (f32[8192,128]{1,0:T(8,128)}, f32[1024,128]{1,0:T(8,128)}) custom-call(f32[8192,128]{1,0:T(8,128)} %bitcast.7, f32[1024,128]{1,0:T(8,128)} %bitcast.9, s32[128,128]{1,0:T(8,128)} %bitcast.11, f32[8]{0:T(128)} %coef.1, s32[8]{0:T(128)} %perm.1, f32[8,8]{1,0:T(8,128)} %constant.11.clone.table, bf16[2,128,160]{2,1,0:T(8,128)(2,1)} %constant.8.clone.near, ...), custom_call_target="tpu_custom_call" | custom-call | flops 2147483648 | bytes 33554432 | tf_op jit(solution)/shard_map/pallas_call | solution.py:410
  103.3 0.0 copy-start
  103.3 4.8 %copy.14 = f32[64,8,16,128]{3,2,1,0:T(8,128)} copy(f32[64,8,16,128]{3,2,1,0:T(8,128)} %bitcast.8) | data formatting | bytes 8388608
  108.1 0.0 copy-done
  108.1 0.8 copy.15
Async XLA Ops:
  103.3 4.8 %copy-start = (f32[1024,128]{1,0:T(8,128)S(1)}, f32[1024,128]{1,0:T(8,128)}, u32[]{:S(2)}) copy-start(f32[1024,128]{1,0:T(8,128)} %get-tuple-element.5) | copy-start | bytes 1572868
